TPU v7x, 32 devices: a whole 2x2x4 slice. The times are simulated.
32 devices in a mesh: dp: 16 (over z, y, x), tensor: 2 (over core).
Axes of the slice: x: 2, y: 2, z: 4, core: 2. Of those that a mesh axis runs over, the one named last changes fastest.
Arguments:
- tokens: bfloat16 [16384, 768], P(('dp', 'tensor')), may hold values from -6 to 6
- lengths: int32 [16], P('dp'), may hold values from 1 to 1024, 10240 in all
- qkv_weight: bfloat16 [3, 768, 768], P(None, 'dp', 'tensor'), may hold values from -0.21875 to 0.21875
- qv_bias: float32 [2, 768], P(None, 'tensor'), may hold values from -3 to 3
- out_weight: bfloat16 [768, 768], P('tensor', 'dp'), may hold values from -0.875 to 0.875
- out_bias: float32 [768], replicated, may hold values from -3 to 3
- up_weight: bfloat16 [768, 3072], P('dp', 'tensor'), may hold values from -0.21875 to 0.21875
- up_bias: float32 [3072], P('tensor'), may hold values from -3 to 3
- down_weight: bfloat16 [3072, 768], P('tensor', 'dp'), may hold values from -0.109375 to 0.109375
- down_bias: float32 [768], replicated, may hold values from -3 to 3
- norm1_gain: float32 [768], replicated, may hold values from 0.5 to 1.5
- norm1_shift: float32 [768], replicated, may hold values from -3 to 3
- norm2_gain: float32 [768], replicated, may hold values from 0.5 to 1.5
- norm2_shift: float32 [768], replicated, may hold values from -3 to 3
- cotangent: bfloat16 [16384, 768], P(('dp', 'tensor')), may hold values from -6 to 6
Outputs:
- layer_output: bfloat16 [16384, 768], P(('dp', 'tensor'))
- input_grad: bfloat16 [16384, 768], P(('dp', 'tensor'))
- grad_qkv_weight: float32 [3, 768, 768], P(None, 'dp', 'tensor')
- grad_qv_bias: float32 [2, 768], P(None, 'tensor')
- grad_out_weight: float32 [768, 768], P('tensor', 'dp')
- grad_out_bias: float32 [768], replicated
- grad_up_weight: float32 [768, 3072], P('dp', 'tensor')
- grad_up_bias: float32 [3072], P('tensor')
- grad_down_weight: float32 [3072, 768], P('tensor', 'dp')
- grad_down_bias: float32 [768], replicated
- grad_norm1_gain: float32 [768], replicated
- grad_norm1_shift: float32 [768], replicated
- grad_norm2_gain: float32 [768], replicated
- grad_norm2_shift: float32 [768], replicated
Inputs may be any that keep to these rules, and one draw needn't show every extreme that they name: lengths[s] is the count of real tokens of sequence s; some sequence has 1024.
All inputs are finite; a program needn't handle non-finite values. No bound on the sum of `lengths` on one device may be relied on, other than what follows from the above.
Results may differ from a plain program's by a relative error of at most 0.017.
Values may be sent and summed in bfloat16 or wider, within the bound.
A program may use at most 192 MiB of HBM per device.

v0:
```python
import jax
import jax.numpy as jnp
from jax import lax
from jax.sharding import PartitionSpec as P

HEAD_DIM = 64
LENGTH = 1024
EPSILON = 1e-05
NEGATIVE = -1e30


def layer_norm(values, norm_gain, norm_shift):
    center = values - jnp.mean(values, axis=-1, keepdims=True)
    spread = jnp.mean(center * center, axis=-1, keepdims=True)
    return center * lax.rsqrt(spread + EPSILON) * norm_gain + norm_shift


def gelu_exact(values):
    return jax.nn.gelu(values, approximate=False)


def matmul(left, right):
    return jnp.dot(left, right, preferred_element_type=jnp.float32)


def contract_rows(left, right):
    return lax.dot_general(
        left, right, (((0,), (0,)), ((), ())), preferred_element_type=jnp.float32
    )


def contract_cols(left, right):
    return lax.dot_general(
        left, right, (((1,), (1,)), ((), ())), preferred_element_type=jnp.float32
    )


def per_device(
    tokens,
    lengths,
    qkv_weight,
    qv_bias,
    out_weight,
    out_bias,
    up_weight,
    up_bias,
    down_weight,
    down_bias,
    norm1_gain,
    norm1_shift,
    norm2_gain,
    norm2_shift,
    cotangent,
):
    tok_rows = tokens.shape[0]
    local_width = qkv_weight.shape[2]
    head_count = local_width // HEAD_DIM
    seq_count = lengths.shape[0]
    block_rows = min(512, LENGTH)
    scaling = HEAD_DIM ** (-0.5)
    positions = jnp.arange(LENGTH)
    qkv_full, out_full, up_full, down_full = (
        lax.all_gather(qkv_weight, "dp", axis=1, tiled=True),
        lax.all_gather(out_weight, "dp", axis=1, tiled=True),
        lax.all_gather(up_weight, "dp", axis=0, tiled=True),
        lax.all_gather(down_weight, "dp", axis=1, tiled=True),
    )
    gathered = lax.all_gather(tokens, "tensor", axis=0, tiled=True)
    queries = (matmul(gathered, qkv_full[0]) + qv_bias[0]).astype(jnp.bfloat16)
    key_rows = matmul(gathered, qkv_full[1]).astype(jnp.bfloat16)
    value_rows = (matmul(gathered, qkv_full[2]) + qv_bias[1]).astype(jnp.bfloat16)

    def forward_seq(packed):
        seq_queries, seq_keys, seq_values, length = packed
        query_heads = seq_queries.reshape(LENGTH, head_count, HEAD_DIM)
        key_heads = seq_keys.reshape(LENGTH, head_count, HEAD_DIM)
        value_heads = seq_values.reshape(LENGTH, head_count, HEAD_DIM)
        usable = (positions < length)[None, None, :]
        context_blocks = []
        total_blocks = []
        for block_start in range(0, LENGTH, block_rows):
            block_q = query_heads[block_start : block_start + block_rows]
            scores = (
                jnp.einsum("qhd,khd->hqk", block_q, key_heads, preferred_element_type=jnp.float32)
                * scaling
            )
            scores = jnp.where(usable, scores, NEGATIVE)
            row_top = jnp.max(scores, axis=-1, keepdims=True)
            exponent = jnp.exp(scores - row_top)
            row_total = jnp.sum(exponent, axis=-1, keepdims=True)
            weights = (exponent / row_total).astype(jnp.bfloat16)
            block_context = jnp.einsum(
                "hqk,khd->qhd", weights, value_heads, preferred_element_type=jnp.float32
            )
            context_blocks.append(block_context.reshape(block_rows, local_width))
            total_blocks.append((row_top + jnp.log(row_total))[..., 0])
        return (
            jnp.concatenate(context_blocks, axis=0).astype(jnp.bfloat16),
            jnp.concatenate(total_blocks, axis=1),
        )

    shaped = (
        queries.reshape(seq_count, LENGTH, local_width),
        key_rows.reshape(seq_count, LENGTH, local_width),
        value_rows.reshape(seq_count, LENGTH, local_width),
    )
    contexts, log_totals = lax.map(forward_seq, (shaped[0], shaped[1], shaped[2], lengths))
    context_flat = contexts.reshape(seq_count * LENGTH, local_width)
    row_block = lax.slice_in_dim(context_flat, 0, tok_rows * lax.axis_size("tensor"), axis=0)
    attn = (
        lax.psum_scatter(matmul(row_block, out_full), "tensor", scatter_dimension=0, tiled=True)
        + out_bias
    )
    first_sum = tokens.astype(jnp.float32) + attn
    hidden = layer_norm(first_sum, norm1_gain, norm1_shift)
    hidden_low = hidden.astype(jnp.bfloat16)
    hidden_all = lax.all_gather(hidden_low, "tensor", axis=0, tiled=True)
    upper = matmul(hidden_all, up_full) + up_bias
    active = gelu_exact(upper).astype(jnp.bfloat16)
    row_block = lax.slice_in_dim(active, 0, tok_rows * lax.axis_size("tensor"), axis=0)
    ffn_out = (
        lax.psum_scatter(matmul(row_block, down_full), "tensor", scatter_dimension=0, tiled=True)
        + down_bias
    )
    second_sum = hidden + ffn_out
    layer_output = layer_norm(second_sum, norm2_gain, norm2_shift).astype(jnp.bfloat16)
    qkv_back, out_back, up_back, down_back = (qkv_full, out_full, up_full, down_full)
    unused_two, norm_two_back = jax.vjp(layer_norm, second_sum, norm2_gain, norm2_shift)
    grad_second, gain_two_grad, shift_two_grad = norm_two_back(cotangent.astype(jnp.float32))
    grad_ffn = grad_second.astype(jnp.bfloat16)
    down_bias_grad = jnp.sum(grad_ffn.astype(jnp.float32), axis=0)
    grad_ffn_all = lax.all_gather(grad_ffn, "tensor", axis=0, tiled=True)
    down_weight_grad = contract_rows(active, grad_ffn_all)
    grad_active = contract_cols(grad_ffn_all, down_back)
    unused_gelu, gelu_back = jax.vjp(gelu_exact, upper)
    grad_upper = gelu_back(grad_active)[0].astype(jnp.bfloat16)
    up_bias_grad = jnp.sum(grad_upper.astype(jnp.float32), axis=0)
    up_weight_grad = contract_rows(hidden_all, grad_upper)
    row_block = lax.slice_in_dim(grad_upper, 0, tok_rows * lax.axis_size("tensor"), axis=0)
    grad_hidden = grad_second + lax.psum_scatter(
        contract_cols(row_block, up_back), "tensor", scatter_dimension=0, tiled=True
    )
    unused_one, norm_one_back = jax.vjp(layer_norm, first_sum, norm1_gain, norm1_shift)
    grad_first, gain_one_grad, shift_one_grad = norm_one_back(grad_hidden)
    grad_attn = grad_first.astype(jnp.bfloat16)
    out_bias_grad = jnp.sum(grad_attn.astype(jnp.float32), axis=0)
    grad_attn_all = lax.all_gather(grad_attn, "tensor", axis=0, tiled=True)
    out_weight_grad = contract_rows(context_flat, grad_attn_all)
    grad_context = contract_cols(grad_attn_all, out_back).astype(jnp.bfloat16)

    def backward_seq(packed):
        seq_queries, seq_keys, seq_values, length, seq_grad, seq_totals = packed
        query_heads = seq_queries.reshape(LENGTH, head_count, HEAD_DIM)
        key_heads = seq_keys.reshape(LENGTH, head_count, HEAD_DIM)
        value_heads = seq_values.reshape(LENGTH, head_count, HEAD_DIM)
        usable = (positions < length)[None, None, :]
        key_grad = jnp.zeros((LENGTH, head_count, HEAD_DIM), jnp.float32)
        value_grad = jnp.zeros((LENGTH, head_count, HEAD_DIM), jnp.float32)
        query_blocks = []
        for block_start in range(0, LENGTH, block_rows):
            block_q = query_heads[block_start : block_start + block_rows]
            block_grad = seq_grad[block_start : block_start + block_rows].reshape(
                block_rows, head_count, HEAD_DIM
            )
            scores = (
                jnp.einsum("qhd,khd->hqk", block_q, key_heads, preferred_element_type=jnp.float32)
                * scaling
            )
            scores = jnp.where(usable, scores, NEGATIVE)
            chances = jnp.exp(scores - seq_totals[:, block_start : block_start + block_rows, None])
            weights = chances.astype(jnp.bfloat16)
            value_grad = value_grad + jnp.einsum(
                "hqk,qhd->khd", weights, block_grad, preferred_element_type=jnp.float32
            )
            grad_weights = jnp.einsum(
                "qhd,khd->hqk", block_grad, value_heads, preferred_element_type=jnp.float32
            )
            inner_sum = jnp.sum(grad_weights * chances, axis=-1, keepdims=True)
            grad_scores = (chances * (grad_weights - inner_sum)).astype(jnp.bfloat16)
            block_query_grad = (
                jnp.einsum(
                    "hqk,khd->qhd", grad_scores, key_heads, preferred_element_type=jnp.float32
                )
                * scaling
            )
            query_blocks.append(block_query_grad.reshape(block_rows, local_width))
            key_grad = (
                key_grad
                + jnp.einsum(
                    "hqk,qhd->khd", grad_scores, block_q, preferred_element_type=jnp.float32
                )
                * scaling
            )
        query_grad = jnp.concatenate(query_blocks, axis=0).astype(jnp.bfloat16)
        return (
            query_grad,
            key_grad.reshape(LENGTH, local_width).astype(jnp.bfloat16),
            value_grad.reshape(LENGTH, local_width).astype(jnp.bfloat16),
        )

    grad_shaped = grad_context.reshape(seq_count, LENGTH, local_width)
    query_grads, key_grads, value_grads = lax.map(
        backward_seq, (shaped[0], shaped[1], shaped[2], lengths, grad_shaped, log_totals)
    )
    query_grads = query_grads.reshape(seq_count * LENGTH, local_width)
    key_grads = key_grads.reshape(seq_count * LENGTH, local_width)
    value_grads = value_grads.reshape(seq_count * LENGTH, local_width)
    qv_bias_grad = jnp.stack(
        [
            jnp.sum(query_grads.astype(jnp.float32), axis=0),
            jnp.sum(value_grads.astype(jnp.float32), axis=0),
        ]
    )
    qkv_weight_grad = jnp.stack(
        [
            contract_rows(gathered, query_grads),
            contract_rows(gathered, key_grads),
            contract_rows(gathered, value_grads),
        ]
    )
    part_query = lax.slice_in_dim(query_grads, 0, lax.axis_size("tensor") * tok_rows, axis=0)
    input_grad = (
        grad_first
        + lax.psum_scatter(
            (
                contract_cols(part_query, qkv_back[0])
                + contract_cols(key_grads, qkv_back[1])
                + contract_cols(value_grads, qkv_back[2])
            ).astype(jnp.bfloat16),
            "tensor",
            scatter_dimension=0,
            tiled=True,
        ).astype(jnp.float32)
    ).astype(jnp.bfloat16)
    qkv_grad_own, out_grad_own, up_grad_own, down_grad_own = (
        lax.psum_scatter(qkv_weight_grad, "dp", scatter_dimension=1, tiled=True),
        lax.psum_scatter(out_weight_grad, "dp", scatter_dimension=1, tiled=True),
        lax.psum_scatter(up_weight_grad, "dp", scatter_dimension=0, tiled=True),
        lax.psum_scatter(down_weight_grad, "dp", scatter_dimension=1, tiled=True),
    )
    qv_bias_total, up_bias_total = lax.psum((qv_bias_grad, up_bias_grad), "dp")
    (
        out_bias_total,
        down_bias_total,
        gain_one_total,
        shift_one_total,
        gain_two_total,
        shift_two_total,
    ) = lax.psum(
        (
            out_bias_grad,
            down_bias_grad,
            gain_one_grad,
            shift_one_grad,
            gain_two_grad,
            shift_two_grad,
        ),
        ("dp", "tensor"),
    )
    return (
        layer_output,
        input_grad,
        qkv_grad_own,
        qv_bias_total,
        out_grad_own,
        out_bias_total,
        up_grad_own,
        up_bias_total,
        down_grad_own,
        down_bias_total,
        gain_one_total,
        shift_one_total,
        gain_two_total,
        shift_two_total,
    )


def solution(mesh):
    return jax.shard_map(
        per_device,
        mesh=mesh,
        in_specs=(
            P(("dp", "tensor"), None),
            P("dp"),
            P(None, "dp", "tensor"),
            P(None, "tensor"),
            P("tensor", "dp"),
            P(),
            P("dp", "tensor"),
            P("tensor"),
            P("tensor", "dp"),
            P(),
            P(),
            P(),
            P(),
            P(),
            P(("dp", "tensor"), None),
        ),
        out_specs=(
            P(("dp", "tensor"), None),
            P(("dp", "tensor"), None),
            P(None, "dp", "tensor"),
            P(None, "tensor"),
            P("tensor", "dp"),
            P(),
            P("dp", "tensor"),
            P("tensor"),
            P("tensor", "dp"),
            P(),
            P(),
            P(),
            P(),
            P(),
        ),
        check_vma=False,
    )
```

profile of v0, /device:TPU:0, one launch (start us, length us, event | category | flops | bytes accessed | tf_op | source)
XLA Modules:
  0.0 1038.2 jit_solution(9922317103957784277)
XLA Ops:
  10.1 49.1 %all_gather.26 = bf16[384,768]{0,1:T(8,128)(2,1)} all-gather(bf16[384,48]{0,1:T(8,128)(2,1)} %param.19), channel_id=1, replica_groups=mesh['dp'=16,'tensor'=2] {'dp'}, dimensions={1}, use_global_device_ids=true | all-gather | bytes 626688 | tf_op jit(solution)/shard_map/all_gather | solution.py:64
  59.2 25.9 %all-gather.10.cloned.1.call-done = bf16[3,768,384]{2,1,0:T(8,128)(2,1)} async-done(((bf16[3,48,384]{2,1,0:T(8,128)(2,1)}), bf16[3,768,384]{2,1,0:T(8,128)(2,1)}) %all-gather.10.cloned.1.call-update) | async-done | bytes 1769488 | tf_op jit(solution)/shard_map/all_gather | solution.py:63
  85.1 2.4 add_convert_fusion.5
  87.6 2.2 convolution_convert_fusion.1
  89.8 1.8 fusion.56
  91.6 4.9 fusion.18
  96.6 5.6 fusion
  102.2 1.9 add_convert_fusion.6
  104.2 3.8 fusion.30
  108.0 3.8 fusion.29
  112.5 2.7 fusion.34
  115.9 9.2 reduce-scatter.8.cloned.1.call-done
  125.1 1.7 fusion.53
  129.2 62.5 %all-gather.14.cloned.1.call-done = bf16[768,1536]{1,0:T(8,128)(2,1)} async-done(((bf16[48,1536]{1,0:T(8,128)(2,1)}), bf16[768,1536]{1,0:T(8,128)(2,1)}) %all-gather.14.cloned.1.call-update) | async-done | bytes 2359312 | tf_op jit(solution)/shard_map/all_gather | solution.py:65
  191.6 10.7 %all-gather.12.cloned.1.call-done = bf16[1024,768]{1,0:T(8,128)(2,1)} async-done(((bf16[512,768]{1,0:T(8,128)(2,1)}), bf16[1024,768]{1,0:T(8,128)(2,1)}) %all-gather.12.cloned.1.call-update) | async-done | bytes 1572880 | tf_op jit(solution)/shard_map/all_gather | solution.py:117
  202.3 19.9 %multiply_convert_fusion.2 = (bf16[1024,1536]{1,0:T(8,128)(2,1)}, f32[1024,1536]{1,0:T(8,128)}, f32[1024,1536]{1,0:T(8,128)}) fusion(f32[1536]{0:T(1024)S(1)} %copy-done.44, bf16[1024,768]{1,0:T(8,128)(2,1)} %all-gather.12.cloned.1.call-done, bf16[768,1536]{1,0:T(8,128)(2,1)} %all-gather.14.cloned.1.call-done), kind=kOutput, calls=%fused_computation.24 | convolution fusion | flops 2519728128 | bytes 19666944 | tf_op jit(solution)/shard_map/dot_general | solution.py:23
  222.2 46.7 %all-gather.16.cloned.1.call-done = bf16[1536,768]{0,1:T(8,128)(2,1)} async-done(((bf16[1536,48]{0,1:T(8,128)(2,1)}), bf16[1536,768]{0,1:T(8,128)(2,1)}) %all-gather.16.cloned.1.call-update) | async-done | bytes 2359312 | tf_op jit(solution)/shard_map/all_gather | solution.py:66
  268.8 6.9 fusion.57
  275.8 9.8 reduce-scatter.10.cloned.1.call-done
  285.6 2.0 fusion.51
  291.5 11.1 %all-gather.18.cloned.1.call-done = bf16[1024,768]{1,0:T(8,128)(2,1)} async-done(((bf16[512,768]{1,0:T(8,128)(2,1)}), bf16[1024,768]{1,0:T(8,128)(2,1)}) %all-gather.18.cloned.1.call-update) | async-done | bytes 1572880 | tf_op jit(solution)/shard_map/all_gather | solution.py:132
  302.5 10.9 %convert_reduce_fusion = (f32[1536]{0:T(1024)}, bf16[1024,1536]{1,0:T(8,128)(2,1)S(1)}) fusion(f32[1024,1536]{1,0:T(8,128)} %get-tuple-element.135, f32[1024,1536]{1,0:T(8,128)} %get-tuple-element.146, f32[1536]{0:T(1024)S(1)} %copy-done.44, bf16[1024,768]{1,0:T(8,128)(2,1)} %all-gather.18.cloned.1.call-done, ...), kind=kOutput, calls=%fused_computation.20 | convolution fusion | flops 2442656256 | bytes 19673088 | tf_op jit(solution)/shard_map/dot_general | solution.py:33
  315.1 4.4 fusion.58
  319.5 12.2 %reduce-scatter.12.cloned.1.call-done = f32[512,768]{1,0:T(8,128)} async-done(((f32[1024,768]{1,0:T(8,128)}), f32[512,768]{1,0:T(8,128)}) %reduce-scatter.12.cloned.1.call-update) | async-done | bytes 1572880 | tf_op jit(solution)/shard_map/reduce_scatter | solution.py:140
  331.7 2.8 multiply_reduce_fusion.2
  338.5 10.6 %all-gather.20.cloned.1.call-done = bf16[1024,768]{1,0:T(8,128)(2,1)} async-done(((bf16[512,768]{1,0:T(8,128)(2,1)}), bf16[1024,768]{1,0:T(8,128)(2,1)}) %all-gather.20.cloned.1.call-update) | async-done | bytes 1572880 | tf_op jit(solution)/shard_map/all_gather | solution.py:147
  349.1 2.2 convolution_convert_fusion
  351.4 6.4 fusion.59
  357.9 7.3 fusion.5
  365.1 18.9 %multiply_reduce_fusion.1 = (f32[6,512]{1,0:T(8,128)S(1)}, f32[6,512]{1,0:T(8,128)S(1)}, f32[6,512,1024]{2,1,0:T(8,128)}) fusion(f32[6,512]{1,0:T(8,128)S(1)} %get-tuple-element.151, f32[6,512,1024]{2,1,0:T(8,128)} %copy-done.1, pred[1024]{0:T(1024)(128)(4,1)S(1)} %iota_compare_fusion, f32[6,512,1024]{2,1,0:T(8,128)} %fusion.59, ...), kind=kOutput, calls=%fused_computation.4 | convolution fusion | flops 434104320 | bytes 51561472 | tf_op jit(solution)/shard_map/while/body/eval_jaxpr/qhd,khd->hqk/dot_general | solution.py:175
  384.1 17.3 %multiply_convert_fusion.1 = (bf16[6,512,1024]{2,1,0:T(8,128)(2,1)S(1)}, bf16[6,512,1024]{2,1,0:T(8,128)(2,1)S(1)}) fusion(f32[6,512,1024]{2,1,0:T(8,128)} %get-tuple-element.147, f32[6,512]{1,0:T(8,128)S(1)} %get-tuple-element.107, f32[6,512]{1,0:T(8,128)S(1)} %get-tuple-element.151, f32[6,512,1024]{2,1,0:T(8,128)} %copy-done.1, ...), kind=kLoop, calls=%fused_computation.3 | loop fusion | flops 37748736 | bytes 62964736 | tf_op jit(solution)/shard_map/while/body/eval_jaxpr/convert_element_type | solution.py:179
  401.4 2.0 fusion.27
  405.0 7.2 convert_reduce_fusion.4
  412.2 2.0 fusion.28
  417.9 2.2 add_convert_fusion.1
  420.2 2.3 convolution_bitcast_fusion.2
  424.3 4.1 copy.30
  429.9 6.3 fusion.62
  436.3 1.8 copy-done.18
  438.1 5.8 fusion.61
  445.0 3.5 fusion.33
  449.8 43.9 %all-reduce.1 = (f32[768]{0:T(1024)}, f32[768]{0:T(1024)}, f32[768]{0:T(1024)}, f32[768]{0:T(1024)}, f32[768]{0:T(1024)}, /*index=5*/f32[768]{0:T(1024)}) all-reduce(f32[768]{0:T(1024)S(1)} %copy-done.30, f32[768]{0:T(1024)S(1)} %get-tuple-element.121, f32[768]{0:T(1024)S(1)} %copy-done.32, ...), channel_id=1, replica_groups=mesh['dp'=16,'tensor'=2] {'dp','tensor'}, use_global_device_ids=true, to_apply=%region_24.25 | all-reduce | flops 4608 | bytes 36864 | tf_op jit(solution)/shard_map/psum | solution.py:249
  494.0 76.4 %all-reduce.2 = (f32[2,384]{1,0:T(2,128)}, f32[1536]{0:T(1024)}) all-reduce(f32[2,384]{1,0:T(2,128)S(1)} %pad_maximum_fusion.7, f32[1536]{0:T(1024)S(1)} %copy-done.34), channel_id=1, replica_groups=mesh['dp'=16,'tensor'=2] {'dp'}, use_global_device_ids=true, to_apply=%region_21.22 | all-reduce | flops 2304 | bytes 18432 | tf_op jit(solution)/shard_map/psum | solution.py:241
  570.5 2.3 add_convert_fusion.2
  572.7 45.6 %all-reduce.5.cloned.1.call-done = f32[3,768,384]{2,0,1:T(4,128)} async-done(((f32[3,768,384]{2,0,1:T(4,128)}), f32[3,768,384]{2,0,1:T(4,128)}) %all-reduce.5.cloned.1.call-update) | async-done | bytes 3538960
  620.1 141.2 %reduce-scatter.20.cloned.1.call-done = f32[1536,48]{0,1:T(8,128)} async-done(((f32[1536,768]{0,1:T(8,128)}), f32[1536,48]{0,1:T(8,128)}) %reduce-scatter.20.cloned.1.call-update) | async-done | bytes 294928 | tf_op jit(solution)/shard_map/reduce_scatter | solution.py:239
  761.2 141.7 %reduce-scatter.18.cloned.1.call-done = f32[48,1536]{1,0:T(8,128)} async-done(((f32[768,1536]{1,0:T(8,128)}), f32[48,1536]{1,0:T(8,128)}) %reduce-scatter.18.cloned.1.call-update) | async-done | bytes 294928 | tf_op jit(solution)/shard_map/reduce_scatter | solution.py:238
  902.9 128.6 %reduce-scatter.16.cloned.1.call-done = f32[384,48]{0,1:T(8,128)} async-done(((f32[384,768]{0,1:T(8,128)}), f32[384,48]{0,1:T(8,128)}) %reduce-scatter.16.cloned.1.call-update) | async-done | bytes 73744 | tf_op jit(solution)/shard_map/reduce_scatter | solution.py:237
  (160 shorter events, 27.8 us)
Async XLA Ops:
  7.2 52.0 %all-gather.8.cloned.1.call-start = ((), (), s32[]{:S(2)}) async-start(), calls=%async_computation.7 | async-start | bytes 2359296 | tf_op jit(solution)/shard_map/all_gather | solution.py:68
  7.9 77.2 %all-gather.10.cloned.1.call-start = ((), (), s32[]{:S(2)}) async-start(), calls=%async_computation.8 | async-start | bytes 1880064 | tf_op jit(solution)/shard_map/all_gather | solution.py:63
  8.7 116.4 %reduce-scatter.8.cloned.1.call-start = ((), (), s32[]{:S(2)}) async-start(), calls=%async_computation.9 | async-start | bytes 4718592 | tf_op jit(solution)/shard_map/reduce_scatter | solution.py:111
  59.2 28.3 %copy-start.40 = (bf16[1024,768]{1,0:T(8,128)(2,1)S(1)}, bf16[1024,768]{1,0:T(8,128)(2,1)}, u32[]{:S(2)}) copy-start(bf16[1024,768]{1,0:T(8,128)(2,1)} %all-gather.8.cloned.1.call-done) | copy-start | bytes 4718596
  87.6 4.1 copy-start.6
  87.6 4.1 copy-start.8
  91.6 16.3 %copy-start = (f32[6,512,1024]{2,1,0:T(8,128)}, f32[6,512,1024]{2,1,0:T(8,128)S(1)}, u32[]{:S(2)}) copy-start(f32[6,512,1024]{2,1,0:T(8,128)S(1)} %fusion.56) | copy-start | bytes 37748740
  96.5 7.6 copy-start.1
  96.6 5.7 copy-start.41
  104.1 3.8 copy-start.19
  107.9 3.8 copy-start.24
  108.0 4.5 copy-start.21
  112.5 12.6 %copy-start.16 = (bf16[512,768]{1,0:T(8,128)(2,1)S(1)}, bf16[512,768]{1,0:T(8,128)(2,1)}, u32[]{:S(2)}) copy-start(bf16[512,768]{1,0:T(8,128)(2,1)} %param.15) | copy-start | bytes 2359300
  112.5 12.6 %copy-start.37 = (f32[768]{0:T(1024)S(1)}, f32[768]{0:T(1024)}, u32[]{:S(2)}) copy-start(f32[768]{0:T(1024)} %param.20) | copy-start | bytes 9220
  115.3 11.8 %copy-start.28 = (f32[768]{0:T(1024)S(1)}, f32[768]{0:T(1024)}, u32[]{:S(2)}) copy-start(f32[768]{0:T(1024)} %param.25) | copy-start | bytes 9220
  115.3 11.8 %copy-start.31 = (f32[768]{0:T(1024)S(1)}, f32[768]{0:T(1024)}, u32[]{:S(2)}) copy-start(f32[768]{0:T(1024)} %param.26) | copy-start | bytes 9220
  115.3 76.3 %all-gather.14.cloned.1.call-start = ((), (), s32[]{:S(2)}) async-start(), calls=%async_computation.11 | async-start | bytes 2506752 | tf_op jit(solution)/shard_map/all_gather | solution.py:65
  115.9 86.4 %all-gather.12.cloned.1.call-start = ((), (), s32[]{:S(2)}) async-start(), calls=%async_computation.10 | async-start | bytes 2359296 | tf_op jit(solution)/shard_map/all_gather | solution.py:117
  126.8 75.5 %copy-start.44 = (f32[1536]{0:T(1024)S(1)}, f32[1536]{0:T(1024)}, u32[]{:S(2)}) copy-start(f32[1536]{0:T(1024)} %param.22) | copy-start | bytes 18436
  128.4 140.5 %all-gather.16.cloned.1.call-start = ((), (), s32[]{:S(2)}) async-start(), calls=%async_computation.12 | async-start | bytes 2506752 | tf_op jit(solution)/shard_map/all_gather | solution.py:66
  128.9 156.7 %reduce-scatter.10.cloned.1.call-start = ((), (), s32[]{:S(2)}) async-start(), calls=%async_computation.13 | async-start | bytes 4718592 | tf_op jit(solution)/shard_map/reduce_scatter | solution.py:122
  275.7 9.9 copy-start.38
  275.7 12.2 %copy-start.14 = (bf16[512,768]{1,0:T(8,128)(2,1)S(1)}, bf16[512,768]{1,0:T(8,128)(2,1)}, u32[]{:S(2)}) copy-start(bf16[512,768]{1,0:T(8,128)(2,1)} %param.29) | copy-start | bytes 2359300
  275.8 12.2 %copy-start.29 = (f32[768]{0:T(1024)S(1)}, f32[768]{0:T(1024)}, u32[]{:S(2)}) copy-start(f32[768]{0:T(1024)} %param.27) | copy-start | bytes 9220
  275.8 26.8 %all-gather.18.cloned.1.call-start = ((), (), s32[]{:S(2)}) async-start(), calls=%async_computation.14 | async-start | bytes 2359296 | tf_op jit(solution)/shard_map/all_gather | solution.py:132
  291.4 40.3 %reduce-scatter.12.cloned.1.call-start = ((), (), s32[]{:S(2)}) async-start(), calls=%async_computation.15 | async-start | bytes 4718592 | tf_op jit(solution)/shard_map/reduce_scatter | solution.py:140
  302.5 12.5 %copy-start.39 = (bf16[768,1536]{1,0:T(8,128)(2,1)S(1)}, bf16[768,1536]{1,0:T(8,128)(2,1)}, u32[]{:S(2)}) copy-start(bf16[768,1536]{1,0:T(8,128)(2,1)} %all-gather.14.cloned.1.call-done) | copy-start | bytes 7077892
  319.5 29.7 %all-gather.20.cloned.1.call-start = ((), (), s32[]{:S(2)}) async-start(), calls=%async_computation.16 | async-start | bytes 2359296 | tf_op jit(solution)/shard_map/all_gather | solution.py:147
  334.5 14.6 %copy-start.22 = (bf16[384,768]{0,1:T(8,128)(2,1)S(1)}, bf16[384,768]{0,1:T(8,128)(2,1)}, u32[]{:S(2)}) copy-start(bf16[384,768]{0,1:T(8,128)(2,1)} %all_gather.26) | copy-start | bytes 1769476
  338.0 13.4 %copy-start.20 = (bf16[1024,384]{0,1:T(8,128)(2,1)S(1)}, bf16[1024,384]{0,1:T(8,128)(2,1)}, u32[]{:S(2)}) copy-start(bf16[1024,384]{0,1:T(8,128)(2,1)} %copy-done.19) | copy-start | bytes 2359300
  338.0 232.5 %reduce-scatter.14.cloned.1.call-start = ((), (), s32[]{:S(2)}) async-start(), calls=%async_computation.17 | async-start | bytes 2359296 | tf_op jit(solution)/shard_map/reduce_scatter | solution.py:224
  384.1 17.3 %copy-start.5 = (bf16[1024,384]{0,1:T(8,128)(2,1)S(1)}, bf16[1024,384]{0,1:T(8,128)(2,1)}, u32[]{:S(2)}) copy-start(bf16[1024,384]{0,1:T(8,128)(2,1)} %copy-done.4) | copy-start | bytes 2359300
  403.5 16.7 %copy-start.10 = (bf16[6,64,512]{2,1,0:T(8,128)(2,1)}, bf16[6,64,512]{2,1,0:T(8,128)(2,1)S(1)}, u32[]{:S(2)}) copy-start(bf16[6,64,512]{2,1,0:T(8,128)(2,1)S(1)} %fusion.27) | copy-start | bytes 1179652
  414.3 6.0 copy-start.12
  420.2 198.2 %all-reduce.5.cloned.1.call-start = ((), (), s32[]{:S(2)}) async-start(), calls=%async_computation.21 | async-start | bytes 9437184
  420.2 2.3 copy-start.42
  428.4 332.8 %reduce-scatter.20.cloned.1.call-start = ((), (), s32[]{:S(2)}) async-start(), calls=%async_computation.20 | async-start | bytes 5013504 | tf_op jit(solution)/shard_map/reduce_scatter | solution.py:239
  436.2 466.7 %reduce-scatter.18.cloned.1.call-start = ((), (), s32[]{:S(2)}) async-start(), calls=%async_computation.19 | async-start | bytes 5013504 | tf_op jit(solution)/shard_map/reduce_scatter | solution.py:238
  443.9 4.6 copy-start.45
  443.9 5.9 copy-start.30
  443.9 5.9 copy-start.32
  443.9 5.9 copy-start.33
  443.9 49.8 %copy-start.36 = (f32[6,64]{1,0:T(8,128)S(1)}, f32[6,64]{1,0:T(8,128)}, u32[]{:S(2)}) copy-start(f32[6,64]{1,0:T(8,128)} %get-tuple-element.148) | copy-start | bytes 4612
  443.9 49.9 %copy-start.11 = (bf16[6,64,512]{2,1,0:T(8,128)(2,1)S(1)}, bf16[6,64,512]{2,1,0:T(8,128)(2,1)}, u32[]{:S(2)}) copy-start(bf16[6,64,512]{2,1,0:T(8,128)(2,1)} %copy-done.10) | copy-start | bytes 1179652
  444.0 49.8 %copy-start.13 = (bf16[6,64,512]{2,1,0:T(8,128)(2,1)S(1)}, bf16[6,64,512]{2,1,0:T(8,128)(2,1)}, u32[]{:S(2)}) copy-start(bf16[6,64,512]{2,1,0:T(8,128)(2,1)} %copy-done.12) | copy-start | bytes 1179652
  444.0 50.0 %copy-start.34 = (f32[1536]{0:T(1024)S(1)}, f32[1536]{0:T(1024)}, u32[]{:S(2)}) copy-start(f32[1536]{0:T(1024)} %get-tuple-element.125) | copy-start | bytes 18436
  444.0 126.5 %copy-start.3 = (f32[512,768]{1,0:T(8,128)S(1)}, f32[512,768]{1,0:T(8,128)}, u32[]{:S(2)}) copy-start(f32[512,768]{1,0:T(8,128)} %copy-done.2) | copy-start | bytes 4718596
  444.0 587.5 %reduce-scatter.16.cloned.1.call-start = ((), (), s32[]{:S(2)}) async-start(), calls=%async_computation.18 | async-start | bytes 1253376 | tf_op jit(solution)/shard_map/reduce_scatter | solution.py:237
  (14 other events, 20.4 us)
Sparse Core Ops, SparseCore 0:
  9.6 12.4 all-gather.7
  24.8 60.2 all-gather.9
  115.4 9.6 reduce-scatter.7
  128.1 63.4 all-gather.13
  193.7 8.6 all-gather.11
  205.3 63.4 all-gather.15
  275.9 9.7 reduce-scatter.9
  291.5 10.9 all-gather.17
  319.6 12.0 reduce-scatter.11
  338.1 10.9 all-gather.19
  420.3 10.2 reduce-scatter.13
  436.1 182.1 all-reduce.4
  624.9 136.2 reduce-scatter.19
  766.8 136.0 reduce-scatter.17
  908.8 122.6 reduce-scatter.15
where the time goes:
time: 1050 us; the launch traced here: 1040 us
  waiting for transfers between devices  658 us (63%)
  blocking collectives  169 us (16%)
  matrix products  138 us (13%)
  other arithmetic  39.6 us (4%)
  between operations  16.1 us (2%)
  local copies, waits for them, and re-layouts  15.8 us (2%)
    reduce_scatter x1, waiting for transfers between devices, per_device(): lax.psum_scatter(up_weight_grad, 'dp', scatter_dimension=0, tiled=True)  142 us
    reduce_scatter x1, waiting for transfers between devices, per_device(): lax.psum_scatter(down_weight_grad, 'dp', scatter_dimension=1, tiled=True)  141 us
    reduce_scatter x1, waiting for transfers between devices, per_device(): lax.psum_scatter(out_weight_grad, 'dp', scatter_dimension=1, tiled=True)  129 us
    psum x1, blocking collectives, per_device(): qv_bias_total, up_bias_total = lax.psum((qv_bias_grad, up_bias_grad), 'dp')  76.4 us
    all_gather x1, waiting for transfers between devices, per_device(): lax.all_gather(up_weight, 'dp', axis=0, tiled=True)  62.5 us
    all_gather x1, blocking collectives, per_device(): lax.all_gather(out_weight, 'dp', axis=1, tiled=True)  49.1 us
    unnamed x16, waiting for transfers between devices  48.2 us
    all_gather x1, waiting for transfers between devices, per_device(): lax.all_gather(down_weight, 'dp', axis=1, tiled=True)  46.7 us
  transfers between devices with their start and end apart: 15, of which 13 were waited for; matrix products, arithmetic and copies ran while one was open for 5% of the time, Pallas kernels for 0%

commit v1 on v0

--- a/solution.py
+++ b/solution.py
@@ -7,6 +7,29 @@
 LENGTH = 1024
 EPSILON = 1e-05
 NEGATIVE = -1e30
+
+
+def arrange_results(q_in, along_axis, dim_no):
+    extra = lax.psum(1, axis_name=along_axis)
+    block_now = lax.axis_index(along_axis)
+    latest, left_arr, earlier = (extra, block_now, q_in.shape[dim_no])
+    bank = tuple((d * latest if c == dim_no else d for c, d in enumerate(q_in.shape)))
+    kept_arr = jnp.zeros(bank, q_in.dtype)
+    w2 = known = q_in
+    v1 = lax.dynamic_update_slice_in_dim(kept_arr, q_in, left_arr * earlier, axis=dim_no)
+    for i0 in range(1, latest // 2 + 1):
+        everything = tuple(((c, (c + 1) % latest) for c in range(latest)))
+        w2 = lax.ppermute(w2, axis_name=along_axis, perm=everything)
+        v1 = lax.dynamic_update_slice_in_dim(
+            v1, w2, (left_arr - i0) % latest * earlier, axis=dim_no
+        )
+        if 2 * i0 < latest:
+            part_next = tuple(((c, (c - 1) % latest) for c in range(latest)))
+            known = lax.ppermute(known, axis_name=along_axis, perm=part_next)
+            v1 = lax.dynamic_update_slice_in_dim(
+                v1, known, (left_arr + i0) % latest * earlier, axis=dim_no
+            )
+    return v1
 
 
 def layer_norm(values, norm_gain, norm_shift):
@@ -60,7 +83,7 @@
     scaling = HEAD_DIM ** (-0.5)
     positions = jnp.arange(LENGTH)
     qkv_full, out_full, up_full, down_full = (
-        lax.all_gather(qkv_weight, "dp", axis=1, tiled=True),
+        arrange_results(qkv_weight, "dp", dim_no=1),
         lax.all_gather(out_weight, "dp", axis=1, tiled=True),
         lax.all_gather(up_weight, "dp", axis=0, tiled=True),
         lax.all_gather(down_weight, "dp", axis=1, tiled=True),

time: 1050 us -> 943 us (0.90)
  waiting for transfers between devices: 658 us -> 523 us
  starting transfers between devices: 1.19 us -> 37.1 us
    reduce_scatter x1, waiting for transfers between devices: 141 us -> 8.11 us  [per_device(): lax.psum_scatter(down_weight_grad, 'dp', scatter_dimension=1, tiled=True)]
    ppermute x0 -> x15, starting transfers between devices: none -> 35.9 us  [the longest x7 33.7 us: arrange_results(): known = lax.ppermute(known, axis_name=along_axis, perm=part_next)]
    ppermute x0 -> x15, waiting for transfers between devices: none -> 29.6 us  [the longest x8 17.2 us: arrange_results(): w2 = lax.ppermute(w2, axis_name=along_axis, perm=everything)]
    all_gather x1 -> x0, waiting for transfers between devices: 25.9 us -> none  [per_device(): lax.all_gather(qkv_weight, 'dp', axis=1, tiled=True)]
    all_gather x1, waiting for transfers between devices: 62.5 us -> 51 us  [per_device(): lax.all_gather(up_weight, 'dp', axis=0, tiled=True)]
    unnamed x16 -> x15, waiting for transfers between devices: 48.2 us -> 57.1 us
  transfers between devices with their start and end apart: 15 -> 29, of which waited for: 13 -> 24; matrix products, arithmetic and copies ran while one was open for 5% -> 6% of each run, Pallas kernels for 0% -> 0%
where the time goes in v1:
time: 943 us; the launch traced here: 939 us
  waiting for transfers between devices  523 us (55%)
  blocking collectives  168 us (18%)
  matrix products  137 us (15%)
  other arithmetic  39.7 us (4%)
  starting transfers between devices  37.1 us (4%)
  between operations  18.3 us (2%)
  local copies, waits for them, and re-layouts  16.4 us (2%)
    reduce_scatter x1, waiting for transfers between devices, per_device(): lax.psum_scatter(up_weight_grad, 'dp', scatter_dimension=0, tiled=True)  142 us
    reduce_scatter x1, waiting for transfers between devices, per_device(): lax.psum_scatter(out_weight_grad, 'dp', scatter_dimension=1, tiled=True)  129 us
    psum x1, blocking collectives, per_device(): qv_bias_total, up_bias_total = lax.psum((qv_bias_grad, up_bias_grad), 'dp')  76.5 us
    unnamed x15, waiting for transfers between devices  57.1 us
    all_gather x1, waiting for transfers between devices, per_device(): lax.all_gather(up_weight, 'dp', axis=0, tiled=True)  51 us
    all_gather x1, blocking collectives, per_device(): lax.all_gather(out_weight, 'dp', axis=1, tiled=True)  47.5 us
    all_gather x1, waiting for transfers between devices, per_device(): lax.all_gather(down_weight, 'dp', axis=1, tiled=True)  46.9 us
    psum x1, blocking collectives, per_device(): lax.psum((out_bias_grad, down_bias_grad, gain_one_grad, shift_one_grad, g...  43.9 us
  transfers between devices with their start and end apart: 29, of which 24 were waited for; matrix products, arithmetic and copies ran while one was open for 6% of the time, Pallas kernels for 0%

profile of v1, /device:TPU:0, one launch (start us, length us, event | category | flops | bytes accessed | tf_op | source)
XLA Modules:
  0.0 939.5 jit_solution(11230341049054929111)
XLA Ops:
  8.1 7.0 collective-permute-start.1
  16.8 47.5 %all_gather.22 = bf16[384,768]{0,1:T(8,128)(2,1)} all-gather(bf16[384,48]{0,1:T(8,128)(2,1)} %param.19), channel_id=1, replica_groups=mesh['dp'=16,'tensor'=2] {'dp'}, dimensions={1}, use_global_device_ids=true | all-gather | bytes 626688 | tf_op jit(solution)/shard_map/all_gather | solution.py:87
  66.7 3.8 collective-permute-done.3
  70.6 2.4 collective-permute-start.5
  75.4 6.1 collective-permute-start.7
  83.8 6.0 collective-permute-start.9
  92.1 6.1 collective-permute-start.11
  100.6 6.0 collective-permute-start.13
  106.8 8.3 collective-permute-done.12
  115.3 8.3 collective-permute-done.14
  123.6 2.9 fusion.26
  129.3 4.9 fusion.18
  134.3 5.6 fusion
  141.9 3.8 fusion.31
  145.7 3.8 fusion.30
  150.2 2.7 fusion.36
  153.6 6.3 reduce-scatter.8.cloned.1.call-done
  164.0 51.0 %all-gather.11.cloned.1.call-done = bf16[768,1536]{1,0:T(8,128)(2,1)} async-done(((bf16[48,1536]{1,0:T(8,128)(2,1)}), bf16[768,1536]{1,0:T(8,128)(2,1)}) %all-gather.11.cloned.1.call-update) | async-done | bytes 2359312 | tf_op jit(solution)/shard_map/all_gather | solution.py:88
  215.0 10.0 %all-gather.9.cloned.1.call-done = bf16[1024,768]{1,0:T(8,128)(2,1)} async-done(((bf16[512,768]{1,0:T(8,128)(2,1)}), bf16[1024,768]{1,0:T(8,128)(2,1)}) %all-gather.9.cloned.1.call-update) | async-done | bytes 1572880 | tf_op jit(solution)/shard_map/all_gather | solution.py:140
  225.1 19.9 %multiply_convert_fusion.2 = (bf16[1024,1536]{1,0:T(8,128)(2,1)}, f32[1024,1536]{1,0:T(8,128)}, f32[1024,1536]{1,0:T(8,128)}) fusion(f32[1536]{0:T(1024)S(1)} %copy-done.46, bf16[1024,768]{1,0:T(8,128)(2,1)} %all-gather.9.cloned.1.call-done, bf16[768,1536]{1,0:T(8,128)(2,1)} %all-gather.11.cloned.1.call-done), kind=kOutput, calls=%fused_computation.24 | convolution fusion | flops 2519728128 | bytes 19666944 | tf_op jit(solution)/shard_map/dot_general | solution.py:46
  245.0 46.9 %all-gather.13.cloned.1.call-done = bf16[1536,768]{0,1:T(8,128)(2,1)} async-done(((bf16[1536,48]{0,1:T(8,128)(2,1)}), bf16[1536,768]{0,1:T(8,128)(2,1)}) %all-gather.13.cloned.1.call-update) | async-done | bytes 2359312 | tf_op jit(solution)/shard_map/all_gather | solution.py:89
  291.9 6.9 fusion.59
  298.9 9.2 reduce-scatter.10.cloned.1.call-done
  314.0 10.9 %all-gather.15.cloned.1.call-done = bf16[1024,768]{1,0:T(8,128)(2,1)} async-done(((bf16[512,768]{1,0:T(8,128)(2,1)}), bf16[1024,768]{1,0:T(8,128)(2,1)}) %all-gather.15.cloned.1.call-update) | async-done | bytes 1572880 | tf_op jit(solution)/shard_map/all_gather | solution.py:155
  324.9 10.9 %convert_reduce_fusion = (f32[1536]{0:T(1024)}, bf16[1024,1536]{1,0:T(8,128)(2,1)S(1)}) fusion(f32[1024,1536]{1,0:T(8,128)} %get-tuple-element.135, f32[1024,1536]{1,0:T(8,128)} %get-tuple-element.146, f32[1536]{0:T(1024)S(1)} %copy-done.46, bf16[1024,768]{1,0:T(8,128)(2,1)} %all-gather.15.cloned.1.call-done, ...), kind=kOutput, calls=%fused_computation.20 | convolution fusion | flops 2442656256 | bytes 19673088 | tf_op jit(solution)/shard_map/dot_general | solution.py:56
  337.5 4.3 fusion.60
  341.9 12.0 %reduce-scatter.12.cloned.1.call-done = f32[512,768]{1,0:T(8,128)} async-done(((f32[1024,768]{1,0:T(8,128)}), f32[512,768]{1,0:T(8,128)}) %reduce-scatter.12.cloned.1.call-update) | async-done | bytes 1572880 | tf_op jit(solution)/shard_map/reduce_scatter | solution.py:163
  354.0 2.8 multiply_reduce_fusion.2
  360.8 10.7 %all-gather.17.cloned.1.call-done = bf16[1024,768]{1,0:T(8,128)(2,1)} async-done(((bf16[512,768]{1,0:T(8,128)(2,1)}), bf16[1024,768]{1,0:T(8,128)(2,1)}) %all-gather.17.cloned.1.call-update) | async-done | bytes 1572880 | tf_op jit(solution)/shard_map/all_gather | solution.py:170
  371.5 2.2 convolution_convert_fusion
  373.8 6.4 fusion.61
  380.2 7.2 fusion.5
  387.5 19.0 %multiply_reduce_fusion.1 = (f32[6,512]{1,0:T(8,128)S(1)}, f32[6,512]{1,0:T(8,128)S(1)}, f32[6,512,1024]{2,1,0:T(8,128)}) fusion(f32[6,512]{1,0:T(8,128)S(1)} %get-tuple-element.151, f32[6,512,1024]{2,1,0:T(8,128)} %copy-done.1, pred[1024]{0:T(1024)(128)(4,1)S(1)} %iota_compare_fusion, f32[6,512,1024]{2,1,0:T(8,128)} %fusion.61, ...), kind=kOutput, calls=%fused_computation.4 | convolution fusion | flops 434104320 | bytes 51561472 | tf_op jit(solution)/shard_map/while/body/eval_jaxpr/qhd,khd->hqk/dot_general | solution.py:198
  406.5 17.3 %multiply_convert_fusion.1 = (bf16[6,512,1024]{2,1,0:T(8,128)(2,1)S(1)}, bf16[6,512,1024]{2,1,0:T(8,128)(2,1)S(1)}) fusion(f32[6,512,1024]{2,1,0:T(8,128)} %get-tuple-element.147, f32[6,512]{1,0:T(8,128)S(1)} %get-tuple-element.107, f32[6,512]{1,0:T(8,128)S(1)} %get-tuple-element.151, f32[6,512,1024]{2,1,0:T(8,128)} %copy-done.1, ...), kind=kLoop, calls=%fused_computation.3 | loop fusion | flops 37748736 | bytes 62964736 | tf_op jit(solution)/shard_map/while/body/eval_jaxpr/convert_element_type | solution.py:202
  427.4 7.2 convert_reduce_fusion.4
  440.3 2.2 add_convert_fusion.1
  442.6 2.3 convolution_bitcast_fusion.2
  446.7 4.0 copy.30
  452.2 6.4 fusion.64
  460.6 5.8 fusion.63
  467.5 3.7 fusion.35
  472.4 43.9 %all-reduce.1 = (f32[768]{0:T(1024)}, f32[768]{0:T(1024)}, f32[768]{0:T(1024)}, f32[768]{0:T(1024)}, f32[768]{0:T(1024)}, /*index=5*/f32[768]{0:T(1024)}) all-reduce(f32[768]{0:T(1024)S(1)} %copy-done.32, f32[768]{0:T(1024)S(1)} %get-tuple-element.121, f32[768]{0:T(1024)S(1)} %copy-done.34, ...), channel_id=1, replica_groups=mesh['dp'=16,'tensor'=2] {'dp','tensor'}, use_global_device_ids=true, to_apply=%region_24.25 | all-reduce | flops 4608 | bytes 36864 | tf_op jit(solution)/shard_map/psum | solution.py:272
  516.6 76.5 %all-reduce.2 = (f32[2,384]{1,0:T(2,128)}, f32[1536]{0:T(1024)}) all-reduce(f32[2,384]{1,0:T(2,128)S(1)} %pad_maximum_fusion.7, f32[1536]{0:T(1024)S(1)} %copy-done.36), channel_id=1, replica_groups=mesh['dp'=16,'tensor'=2] {'dp'}, use_global_device_ids=true, to_apply=%region_21.22 | all-reduce | flops 2304 | bytes 18432 | tf_op jit(solution)/shard_map/psum | solution.py:264
  593.1 2.3 add_convert_fusion.2
  595.4 55.9 %all-reduce.5.cloned.1.call-done = f32[3,768,384]{2,0,1:T(4,128)} async-done(((f32[3,768,384]{2,0,1:T(4,128)}), f32[3,768,384]{2,0,1:T(4,128)}) %all-reduce.5.cloned.1.call-update) | async-done | bytes 3538960
  653.0 8.1 reduce-scatter.20.cloned.1.call-done
  661.1 141.9 %reduce-scatter.18.cloned.1.call-done = f32[48,1536]{1,0:T(8,128)} async-done(((f32[768,1536]{1,0:T(8,128)}), f32[48,1536]{1,0:T(8,128)}) %reduce-scatter.18.cloned.1.call-update) | async-done | bytes 294928 | tf_op jit(solution)/shard_map/reduce_scatter | solution.py:261
  803.0 128.9 %reduce-scatter.16.cloned.1.call-done = f32[384,48]{0,1:T(8,128)} async-done(((f32[384,768]{0,1:T(8,128)}), f32[384,48]{0,1:T(8,128)}) %reduce-scatter.16.cloned.1.call-update) | async-done | bytes 73744 | tf_op jit(solution)/shard_map/reduce_scatter | solution.py:260
  (208 shorter events, 52.8 us)
Async XLA Ops:
  8.0 56.5 %copy-start.29 = (bf16[3,48,384]{2,1,0:T(8,128)(2,1)S(1)}, bf16[3,48,384]{2,1,0:T(8,128)(2,1)}, u32[]{:S(2)}) copy-start(bf16[3,48,384]{2,1,0:T(8,128)(2,1)} %param.17) | copy-start | bytes 331780
  8.0 115.6 %all-gather.7.cloned.1.call-start = ((), (), s32[]{:S(2)}) async-start(), calls=%async_computation.7 | async-start | bytes 2359296 | tf_op jit(solution)/shard_map/all_gather | solution.py:91
  8.1 56.5 %collective-permute-start.1 = (bf16[3,48,384]{2,1,0:T(8,128)(2,1)}, bf16[3,48,384]{2,1,0:T(8,128)(2,1)S(1)}, u32[]{:S(2)}, u32[]{:S(2)}) collective-permute-start(bf16[3,48,384]{2,1,0:T(8,128)(2,1)} %param.17), channel_id=1, source_target_pairs={{0,30},{2,0},{4,2},{6,4},{8,6},{10,8},{12,10},{14,12},{16,14},{18,... | collective-permute-start | bytes 331784 | tf_op jit(solution)/shard_map/ppermute | solution.py:28
  15.1 49.6 %collective-permute-start = (bf16[3,48,384]{2,1,0:T(8,128)(2,1)}, bf16[3,48,384]{2,1,0:T(8,128)(2,1)S(1)}, u32[]{:S(2)}, u32[]{:S(2)}) collective-permute-start(bf16[3,48,384]{2,1,0:T(8,128)(2,1)} %param.17), channel_id=1, source_target_pairs={{0,2},{2,4},{4,6},{6,8},{8,10},{10,12},{12,14},{14,16},{16,18},{18... | collective-permute-start | bytes 331784 | tf_op jit(solution)/shard_map/ppermute | solution.py:22
  15.1 144.8 %reduce-scatter.8.cloned.1.call-start = ((), (), s32[]{:S(2)}) async-start(), calls=%async_computation.8 | async-start | bytes 4718592 | tf_op jit(solution)/shard_map/reduce_scatter | solution.py:134
  64.6 6.0 collective-permute-start.3
  64.7 8.5 collective-permute-start.2
  70.6 4.8 collective-permute-start.5
  73.1 8.5 collective-permute-start.4
  75.4 8.4 collective-permute-start.7
  81.6 8.3 collective-permute-start.6
  83.8 8.3 collective-permute-start.9
  89.9 8.4 collective-permute-start.8
  92.1 8.4 collective-permute-start.11
  98.4 8.3 collective-permute-start.10
  100.6 14.7 %collective-permute-start.13 = (bf16[3,48,384]{2,1,0:T(8,128)(2,1)S(1)}, bf16[3,48,384]{2,1,0:T(8,128)(2,1)S(1)}, u32[]{:S(2)}, u32[]{:S(2)}) collective-permute-start(bf16[3,48,384]{2,1,0:T(8,128)(2,1)S(1)} %collective-permute-done.11), channel_id=1, source_target_pairs={{0,30},{2,0},{4,2},{6,4},{8,6},{10,8},{12,10},{14,12},{16,14},{18,... | collective-permute-start | bytes 331784 | tf_op jit(solution)/shard_map/ppermute | solution.py:28
  106.7 8.3 collective-permute-start.12
  115.1 8.5 collective-permute-start.14
  129.3 16.3 %copy-start = (f32[6,512,1024]{2,1,0:T(8,128)}, f32[6,512,1024]{2,1,0:T(8,128)S(1)}, u32[]{:S(2)}) copy-start(f32[6,512,1024]{2,1,0:T(8,128)S(1)} %fusion.58) | copy-start | bytes 37748740
  150.2 9.7 %copy-start.18 = (bf16[512,768]{1,0:T(8,128)(2,1)S(1)}, bf16[512,768]{1,0:T(8,128)(2,1)}, u32[]{:S(2)}) copy-start(bf16[512,768]{1,0:T(8,128)(2,1)} %param.15) | copy-start | bytes 2359300
  150.2 9.7 %copy-start.39 = (f32[768]{0:T(1024)S(1)}, f32[768]{0:T(1024)}, u32[]{:S(2)}) copy-start(f32[768]{0:T(1024)} %param.20) | copy-start | bytes 9220
  153.0 9.0 copy-start.30
  153.0 62.1 %all-gather.11.cloned.1.call-start = ((), (), s32[]{:S(2)}) async-start(), calls=%async_computation.10 | async-start | bytes 2506752 | tf_op jit(solution)/shard_map/all_gather | solution.py:88
  153.6 71.5 %all-gather.9.cloned.1.call-start = ((), (), s32[]{:S(2)}) async-start(), calls=%async_computation.9 | async-start | bytes 2359296 | tf_op jit(solution)/shard_map/all_gather | solution.py:140
  161.6 63.5 %copy-start.46 = (f32[1536]{0:T(1024)S(1)}, f32[1536]{0:T(1024)}, u32[]{:S(2)}) copy-start(f32[1536]{0:T(1024)} %param.22) | copy-start | bytes 18436
  163.2 128.7 %all-gather.13.cloned.1.call-start = ((), (), s32[]{:S(2)}) async-start(), calls=%async_computation.11 | async-start | bytes 2506752 | tf_op jit(solution)/shard_map/all_gather | solution.py:89
  163.8 144.3 %reduce-scatter.10.cloned.1.call-start = ((), (), s32[]{:S(2)}) async-start(), calls=%async_computation.12 | async-start | bytes 4718592 | tf_op jit(solution)/shard_map/reduce_scatter | solution.py:145
  298.8 9.3 copy-start.40
  298.8 11.6 %copy-start.16 = (bf16[512,768]{1,0:T(8,128)(2,1)S(1)}, bf16[512,768]{1,0:T(8,128)(2,1)}, u32[]{:S(2)}) copy-start(bf16[512,768]{1,0:T(8,128)(2,1)} %param.29) | copy-start | bytes 2359300
  298.8 11.6 %copy-start.31 = (f32[768]{0:T(1024)S(1)}, f32[768]{0:T(1024)}, u32[]{:S(2)}) copy-start(f32[768]{0:T(1024)} %param.27) | copy-start | bytes 9220
  298.8 26.1 %all-gather.15.cloned.1.call-start = ((), (), s32[]{:S(2)}) async-start(), calls=%async_computation.13 | async-start | bytes 2359296 | tf_op jit(solution)/shard_map/all_gather | solution.py:155
  314.0 40.0 %reduce-scatter.12.cloned.1.call-start = ((), (), s32[]{:S(2)}) async-start(), calls=%async_computation.14 | async-start | bytes 4718592 | tf_op jit(solution)/shard_map/reduce_scatter | solution.py:163
  324.9 12.6 %copy-start.41 = (bf16[768,1536]{1,0:T(8,128)(2,1)S(1)}, bf16[768,1536]{1,0:T(8,128)(2,1)}, u32[]{:S(2)}) copy-start(bf16[768,1536]{1,0:T(8,128)(2,1)} %all-gather.11.cloned.1.call-done) | copy-start | bytes 7077892
  341.9 29.6 %all-gather.17.cloned.1.call-start = ((), (), s32[]{:S(2)}) async-start(), calls=%async_computation.15 | async-start | bytes 2359296 | tf_op jit(solution)/shard_map/all_gather | solution.py:170
  356.8 14.7 %copy-start.24 = (bf16[384,768]{0,1:T(8,128)(2,1)S(1)}, bf16[384,768]{0,1:T(8,128)(2,1)}, u32[]{:S(2)}) copy-start(bf16[384,768]{0,1:T(8,128)(2,1)} %all_gather.22) | copy-start | bytes 1769476
  360.3 13.5 %copy-start.22 = (bf16[384,1024]{1,0:T(8,128)(2,1)S(1)}, bf16[384,1024]{1,0:T(8,128)(2,1)}, u32[]{:S(2)}) copy-start(bf16[384,1024]{1,0:T(8,128)(2,1)} %copy-done.21) | copy-start | bytes 2359300
  360.3 232.9 %reduce-scatter.14.cloned.1.call-start = ((), (), s32[]{:S(2)}) async-start(), calls=%async_computation.16 | async-start | bytes 2359296 | tf_op jit(solution)/shard_map/reduce_scatter | solution.py:247
  406.5 17.3 %copy-start.5 = (bf16[384,1024]{1,0:T(8,128)(2,1)S(1)}, bf16[384,1024]{1,0:T(8,128)(2,1)}, u32[]{:S(2)}) copy-start(bf16[384,1024]{1,0:T(8,128)(2,1)} %copy-done.4) | copy-start | bytes 2359300
  425.8 16.7 %copy-start.12 = (bf16[6,64,512]{2,1,0:T(8,128)(2,1)}, bf16[6,64,512]{2,1,0:T(8,128)(2,1)S(1)}, u32[]{:S(2)}) copy-start(bf16[6,64,512]{2,1,0:T(8,128)(2,1)S(1)} %fusion.28) | copy-start | bytes 1179652
  442.5 208.7 %all-reduce.5.cloned.1.call-start = ((), (), s32[]{:S(2)}) async-start(), calls=%async_computation.20 | async-start | bytes 9437184
  450.8 210.3 %reduce-scatter.20.cloned.1.call-start = ((), (), s32[]{:S(2)}) async-start(), calls=%async_computation.19 | async-start | bytes 5013504 | tf_op jit(solution)/shard_map/reduce_scatter | solution.py:262
  458.7 344.3 %reduce-scatter.18.cloned.1.call-start = ((), (), s32[]{:S(2)}) async-start(), calls=%async_computation.18 | async-start | bytes 5013504 | tf_op jit(solution)/shard_map/reduce_scatter | solution.py:261
  466.4 49.9 %copy-start.38 = (f32[6,64]{1,0:T(8,128)S(1)}, f32[6,64]{1,0:T(8,128)}, u32[]{:S(2)}) copy-start(f32[6,64]{1,0:T(8,128)} %get-tuple-element.148) | copy-start | bytes 4612
  466.4 49.9 %copy-start.13 = (bf16[6,64,512]{2,1,0:T(8,128)(2,1)S(1)}, bf16[6,64,512]{2,1,0:T(8,128)(2,1)}, u32[]{:S(2)}) copy-start(bf16[6,64,512]{2,1,0:T(8,128)(2,1)} %copy-done.12) | copy-start | bytes 1179652
  466.4 49.9 %copy-start.15 = (bf16[6,64,512]{2,1,0:T(8,128)(2,1)S(1)}, bf16[6,64,512]{2,1,0:T(8,128)(2,1)}, u32[]{:S(2)}) copy-start(bf16[6,64,512]{2,1,0:T(8,128)(2,1)} %copy-done.14) | copy-start | bytes 1179652
  466.5 50.1 %copy-start.36 = (f32[1536]{0:T(1024)S(1)}, f32[1536]{0:T(1024)}, u32[]{:S(2)}) copy-start(f32[1536]{0:T(1024)} %get-tuple-element.125) | copy-start | bytes 18436
  466.5 126.7 %copy-start.3 = (f32[512,768]{1,0:T(8,128)S(1)}, f32[512,768]{1,0:T(8,128)}, u32[]{:S(2)}) copy-start(f32[512,768]{1,0:T(8,128)} %copy-done.2) | copy-start | bytes 4718596
  466.5 465.4 %reduce-scatter.16.cloned.1.call-start = ((), (), s32[]{:S(2)}) async-start(), calls=%async_computation.17 | async-start | bytes 1253376 | tf_op jit(solution)/shard_map/reduce_scatter | solution.py:260
  (30 other events, 98.3 us)
Sparse Core Ops, SparseCore 0:
  15.2 11.1 all-gather.6
  153.1 6.7 reduce-scatter.7
  298.9 9.1 reduce-scatter.9
  360.4 11.0 all-gather.16
  442.7 10.2 reduce-scatter.13
  459.3 201.6 reduce-scatter.19
  666.8 136.1 reduce-scatter.17
  809.0 122.7 reduce-scatter.15
Sparse Core Ops, SparseCore 1:
  156.6 58.3 all-gather.10
  217.1 7.9 all-gather.8
  228.2 63.7 all-gather.12
  314.0 10.8 all-gather.14
  342.0 11.9 reduce-scatter.11
  450.9 200.3 all-reduce.4
